TPU v7x, 128 devices: a whole 4x4x4 slice. The times are simulated.
128 devices in a mesh: phase: 4 (over x), grp: 4 (over z_hi, core), tp: 8 (over z_lo, y).
Axes of the slice: x: 4, y: 4, z: 4 (z_hi: 2, z_lo: 2; z = z_hi * 2 + z_lo), core: 2. Of those that a mesh axis runs over, the one named last changes fastest.
Arguments:
- prompt_embed: bfloat16 [512, 8192], P('grp', 'tp'), may hold values from -6 to 6
- prompt_lengths: int32 [4, 4], replicated, may hold values from 1 to 64, 128 in all within a row
- decode_group: int32 [4, 4, 1], replicated, may hold values from 0 to 3; in each aligned block of 4 rows (0 to 3, 4 to 7, ..., all dimensions but the last counted through in order) at most 2 rows name the same one
- step_embed: bfloat16 [4, 16, 8192], P(None, 'grp', 'tp'), may hold values from -6 to 6
- norm_gain: float32 [4, 8192], P('phase'), may hold values from 0.5 to 1.5
- w_query: bfloat16 [4, 8192, 4096], P('phase', None, 'tp'), may hold values from -0.0625 to 0.0625
- w_key: bfloat16 [4, 8192, 1024], P('phase', None, 'tp'), may hold values from -0.0625 to 0.0625
- w_value: bfloat16 [4, 8192, 1024], P('phase', None, 'tp'), may hold values from -0.0625 to 0.0625
- w_out: bfloat16 [4, 4096, 8192], P('phase', 'tp'), may hold values from -0.09375 to 0.09375
Outputs:
- prefill_out: bfloat16 [4, 512, 8192], P('phase', 'grp', 'tp')
- decode_out: bfloat16 [4, 4, 32, 8192], P('phase', None, 'grp', 'tp')
Inputs may be any that keep to these rules, and one draw needn't show every extreme that they name: `prompt_lengths`: the 4 prompts of one prefill device fill its 128 rows; the longest has 64 tokens. `decode_group`: at most 2 prompts of one prefill device go to the same decode device, and some device sends exactly 2 to one.
All inputs are finite; a program needn't handle non-finite values.
Results may differ from a plain program's by a relative error of at most 0.023.
Values may be sent and summed in bfloat16 or wider, within the bound.
A program may use at most 128 MiB of HBM per device.

v0:
```python
import math

import jax
import jax.numpy as jnp
from jax import lax
from jax.sharding import PartitionSpec as P

HQ = 32
KVH = 8
HD = 128
BLK = 128
CAP = 2
STEPS = 4
MAXLEN = 64


EPS = 1e-06
THETA = 1000000.0


def shifted(value, axis, steps):
    count = lax.axis_size(axis)
    initial, last = (max(0, -steps), min(count, count - steps))
    return lax.ppermute(value, axis, [(source, source + steps) for source in range(initial, last)])


def rotate(values, places):
    half_dim = values.shape[-1] // 2
    frequency = THETA ** (-2.0 * jnp.arange(half_dim, dtype=jnp.float32) / values.shape[-1])
    angles = places[..., None, None] * frequency
    cosine = jnp.cos(angles)
    sine_part = jnp.sin(angles)
    first_half = values[..., :half_dim]
    second_half = values[..., half_dim:]
    return jnp.concatenate(
        [
            first_half * cosine - second_half * sine_part,
            second_half * cosine + first_half * sine_part,
        ],
        axis=-1,
    )


def normed(hidden, gain_row):
    values = hidden.astype(jnp.float32)
    factor = lax.rsqrt(jnp.mean(values * values, axis=-1, keepdims=True) + EPS)
    return (values * factor * gain_row).astype(jnp.bfloat16)


def softmax_rows(scores, allowed):
    masked = jnp.where(allowed, scores, -1e30)
    return jax.nn.softmax(masked, axis=-1).astype(jnp.bfloat16)


def project_in(entering, gain_row, query_w, key_w, value_w):
    whole_rows = lax.all_gather(entering, "tp", axis=1, tiled=True)
    normal_rows = normed(whole_rows, gain_row)
    queries = jnp.dot(normal_rows, query_w, preferred_element_type=jnp.float32)
    new_keys = jnp.dot(normal_rows, key_w, preferred_element_type=jnp.float32)
    new_values = jnp.dot(normal_rows, value_w, preferred_element_type=jnp.float32)
    return (whole_rows, queries, new_keys, new_values)


def project_out(entering, head_out, out_w):
    partial_sum = jnp.dot(head_out, out_w, preferred_element_type=jnp.float32)
    share_part = lax.psum_scatter(
        partial_sum.astype(jnp.bfloat16), "tp", scatter_dimension=1, tiled=True
    ).astype(jnp.float32)
    result = (entering.astype(jnp.float32) + share_part).astype(jnp.bfloat16)
    return (result, result)


def pass_on(carried):
    return shifted(carried, "phase", 1)


def body(
    prompt_embed,
    prompt_lengths,
    decode_group,
    step_embed,
    norm_gain,
    w_query,
    w_key,
    w_value,
    w_out,
):
    n_grp = lax.axis_size("grp")
    n_phase = lax.axis_size("phase")
    phase_idx = lax.axis_index("phase")
    source = lax.axis_index("grp")
    gain_row = norm_gain[0]
    query_w = w_query[0]
    key_w = w_key[0]
    value_w = w_value[0]
    out_w = w_out[0]
    per_group = HQ // KVH
    local_kv = key_w.shape[1] // HD
    local_q = query_w.shape[1] // HD
    score_scale = 1.0 / math.sqrt(HD)
    ptok = prompt_embed.shape[0]
    shard_width = prompt_embed.shape[1]
    blocks = ptok // BLK
    docs = prompt_lengths.shape[1]
    all_ends = jnp.cumsum(prompt_lengths, axis=1)
    all_starts = all_ends - prompt_lengths
    lengths = prompt_lengths[source]
    doc_ends = all_ends[source]
    starts = all_starts[source]
    places = jnp.arange(ptok, dtype=jnp.int32)
    segment = jnp.sum((places[:, None] >= doc_ends[None, :]).astype(jnp.int32), axis=-1)
    positions = (places - starts[segment]).astype(jnp.float32)
    width_in = prompt_embed.shape[1]

    def prefill_round(current, carry):
        incoming, key_buf, value_buf, out_buf = carry
        block_idx = current - phase_idx
        usable = (block_idx >= 0) & (block_idx < blocks)
        first_row = jnp.clip(block_idx, 0, blocks - 1) * BLK
        entering = jnp.where(phase_idx == 0, prompt_embed, incoming)
        whole_rows, queries, new_keys, new_values = project_in(
            entering, gain_row, query_w, key_w, value_w
        )
        queries = (
            rotate(queries.reshape(BLK, local_q, HD), positions)
            .astype(jnp.bfloat16)
            .reshape(BLK, local_kv, per_group, HD)
        )
        new_keys = (
            rotate(new_keys.reshape(BLK, local_kv, HD), positions)
            .astype(jnp.bfloat16)
            .reshape(BLK, local_kv * HD)
        )
        new_values = new_values.astype(jnp.bfloat16)
        key_buf = jnp.where(usable, new_keys, key_buf)
        value_buf = jnp.where(usable, new_values, value_buf)
        block_rows = first_row + jnp.arange(BLK, dtype=jnp.int32)
        allowed = (segment[:, None] == segment[None, :]) & (block_rows[:, None] >= places[None, :])
        scores = (
            jnp.einsum(
                "qkgd,skd->kgqs",
                queries,
                key_buf.reshape(ptok, local_kv, HD),
                preferred_element_type=jnp.float32,
            )
            * score_scale
        )
        probability = softmax_rows(scores, allowed[None, None])
        head_out = jnp.einsum(
            "kgqs,skd->qkgd",
            probability,
            value_buf.reshape(ptok, local_kv, HD),
            preferred_element_type=jnp.float32,
        )
        head_out = head_out.astype(jnp.bfloat16).reshape(BLK, local_q * HD)
        carried, out_shard = project_out(entering, head_out, out_w)
        out_buf = jnp.where(usable, out_shard, out_buf)
        return (pass_on(carried), key_buf, value_buf, out_buf)

    start_carry = (
        jnp.zeros((BLK, width_in), jnp.bfloat16),
        jnp.zeros((ptok, local_kv * HD), jnp.bfloat16),
        jnp.zeros((ptok, local_kv * HD), jnp.bfloat16),
        jnp.zeros((ptok, shard_width), jnp.bfloat16),
    )
    passed, key_buf, value_buf, prefill_buf = lax.fori_loop(
        0, blocks + n_phase - 1, prefill_round, start_carry
    )
    assign = decode_group[:, :, 0]
    doc_ids = jnp.arange(docs, dtype=jnp.int32)
    earlier = doc_ids[:, None] > doc_ids[None, :]
    slot_rank = jnp.sum(
        ((assign[:, :, None] == assign[:, None, :]) & earlier[None]).astype(jnp.int32), axis=-1
    )
    dest_ids = jnp.arange(n_grp, dtype=jnp.int32)
    cap_ids = jnp.arange(CAP, dtype=jnp.int32)
    selector = (assign[:, None, None, :] == dest_ids[None, :, None, None]) & (
        slot_rank[:, None, None, :] == cap_ids[None, None, :, None]
    )
    arriving = jnp.take(selector, source, axis=1).astype(jnp.int32)
    slot_len = jnp.sum(arriving * prompt_lengths[:, None, :], axis=-1).reshape(-1)
    slot_live = jnp.sum(arriving, axis=-1).reshape(-1) > 0
    offset = jnp.arange(MAXLEN, dtype=jnp.int32)
    slot_inside = offset[None, :] < slot_len[:, None]
    row_ids = jnp.minimum(starts[:, None] + offset[None, :], ptok - 1)
    doc_inside = offset[None, :] < lengths[:, None]
    doc_keys = jnp.where(doc_inside[:, :, None], key_buf[row_ids], jnp.zeros((), jnp.bfloat16))
    doc_values = jnp.where(doc_inside[:, :, None], value_buf[row_ids], jnp.zeros((), jnp.bfloat16))
    outgoing = jnp.take(selector, source, axis=0).astype(jnp.bfloat16)
    send_keys = jnp.einsum(
        "acd,dmx->acmx", outgoing, doc_keys, preferred_element_type=jnp.float32
    ).astype(jnp.bfloat16)
    send_values = jnp.einsum(
        "acd,dmx->acmx", outgoing, doc_values, preferred_element_type=jnp.float32
    ).astype(jnp.bfloat16)
    send_steps = jnp.einsum(
        "acd,jdx->acjx", outgoing, step_embed, preferred_element_type=jnp.float32
    ).astype(jnp.bfloat16)
    got_keys, got_values, got_steps = (
        lax.all_to_all(send_keys, "grp", split_axis=0, concat_axis=0, tiled=True),
        lax.all_to_all(send_values, "grp", split_axis=0, concat_axis=0, tiled=True),
        lax.all_to_all(send_steps, "grp", split_axis=0, concat_axis=0, tiled=True),
    )
    slot_keys = got_keys.reshape(-1, MAXLEN, local_kv * HD)
    slot_values = got_values.reshape(-1, MAXLEN, local_kv * HD)
    slot_steps = got_steps.reshape(-1, STEPS, shard_width)
    slot_count = slot_keys.shape[0]
    slot_keys = slot_keys.reshape(slot_count, MAXLEN, local_kv, HD)
    slot_values = slot_values.reshape(slot_count, MAXLEN, local_kv, HD)
    step_ids = jnp.arange(STEPS, dtype=jnp.int32)

    def decode_round(current, carry):
        incoming, fresh_keys, fresh_values, out_buf = carry
        step_idx = current - phase_idx
        usable = (step_idx >= 0) & (step_idx < STEPS)
        which_step = jnp.clip(step_idx, 0, STEPS - 1)
        native = lax.dynamic_index_in_dim(slot_steps, which_step, 1, keepdims=False)
        entering = jnp.where(phase_idx == 0, native, incoming)
        whole_rows, queries, new_key, new_value = project_in(
            entering, gain_row, query_w, key_w, value_w
        )
        places_now = (slot_len + which_step).astype(jnp.float32)
        queries = (
            rotate(queries.reshape(slot_count, local_q, HD), places_now)
            .astype(jnp.bfloat16)
            .reshape(slot_count, local_kv, per_group, HD)
        )
        new_key = rotate(new_key.reshape(slot_count, local_kv, HD), places_now).astype(jnp.bfloat16)
        new_value = new_value.astype(jnp.bfloat16).reshape(slot_count, local_kv, HD)
        fresh_keys = jnp.where(
            usable,
            lax.dynamic_update_slice_in_dim(fresh_keys, new_key[:, None], which_step, 1),
            fresh_keys,
        )
        fresh_values = jnp.where(
            usable,
            lax.dynamic_update_slice_in_dim(fresh_values, new_value[:, None], which_step, 1),
            fresh_values,
        )
        all_keys = jnp.concatenate([slot_keys, fresh_keys], axis=1)
        all_values = jnp.concatenate([slot_values, fresh_values], axis=1)
        allowed = jnp.concatenate(
            [slot_inside, jnp.broadcast_to(step_ids[None, :] <= which_step, (slot_count, STEPS))],
            axis=1,
        )
        scores = (
            jnp.einsum("skgd,smkd->skgm", queries, all_keys, preferred_element_type=jnp.float32)
            * score_scale
        )
        probability = softmax_rows(scores, allowed[:, None, None])
        head_out = jnp.einsum(
            "skgm,smkd->skgd", probability, all_values, preferred_element_type=jnp.float32
        )
        head_out = head_out.astype(jnp.bfloat16).reshape(slot_count, local_q * HD)
        carried, out_shard = project_out(entering, head_out, out_w)
        out_buf = jnp.where(
            usable,
            lax.dynamic_update_slice_in_dim(out_buf, out_shard[None], which_step, 0),
            out_buf,
        )
        return (pass_on(carried), fresh_keys, fresh_values, out_buf)

    decode_start = (
        jnp.zeros((slot_count, slot_steps.shape[2]), jnp.bfloat16),
        jnp.zeros((slot_count, STEPS, local_kv, HD), jnp.bfloat16),
        jnp.zeros((slot_count, STEPS, local_kv, HD), jnp.bfloat16),
        jnp.zeros((STEPS, slot_count, shard_width), jnp.bfloat16),
    )
    passed, fresh_keys, fresh_values, decode_buf = lax.fori_loop(
        0, STEPS + n_phase - 1, decode_round, decode_start
    )
    decode_buf = jnp.where(slot_live[None, :, None], decode_buf, jnp.zeros((), jnp.bfloat16))
    return (prefill_buf[None], decode_buf[None])


def solution(mesh):
    return jax.shard_map(
        body,
        mesh=mesh,
        in_specs=(
            P("grp", "tp"),
            P(),
            P(),
            P(None, "grp", "tp"),
            P("phase", None),
            P("phase", None, "tp"),
            P("phase", None, "tp"),
            P("phase", None, "tp"),
            P("phase", "tp", None),
        ),
        out_specs=(P("phase", "grp", "tp"), P("phase", None, "grp", "tp")),
        check_vma=False,
    )
```

profile of v0, /device:TPU:7, one launch (start us, length us, event | category | flops | bytes accessed | tf_op | source)
XLA Modules:
  0.0 1108.1 jit_solution(13848321263904834064)
XLA Ops:
  9.7 5.8 all-to-all-start
  21.3 455.7 %while.47 = (s32[]{:T(128)}, bf16[128,1024]{1,0:T(8,128)(2,1)S(1)}, bf16[128,128]{1,0:T(8,128)(2,1)S(1)}, bf16[128,128]{1,0:T(8,128)(2,1)S(1)}, bf16[128,1024]{1...) while((s32[]{:T(128)}, bf16[128,1024]{1,0:T(8,128)(2,1)S(1)}, ...), condition=%wide.region_7.8_spmd.clone, body=%wide.region_2.7_spmd.clone.sunk | while | flops 2736995840 | bytes 70271720 | solution.py:166
  22.6 39.8 %all-gather.2.cloned.1.call-done = bf16[128,8192]{1,0:T(8,128)(2,1)} async-done(((bf16[128,1024]{1,0:T(8,128)(2,1)}), bf16[128,8192]{1,0:T(8,128)(2,1)}) %all-gather.2.cloned.1.call-update) | async-done | bytes 2097168 | tf_op jit(solution)/shard_map/while/body/eval_jaxpr/all_gather | solution.py:56
  76.4 6.1 convolution_convert_fusion.13
  82.5 41.7 %reduce-scatter.3.cloned.1.call-done = bf16[128,1024]{1,0:T(8,128)(2,1)} async-done(((bf16[128,8192]{1,0:T(8,128)(2,1)}), bf16[128,1024]{1,0:T(8,128)(2,1)}) %reduce-scatter.3.cloned.1.call-update) | async-done | bytes 262160 | tf_op jit(solution)/shard_map/while/body/eval_jaxpr/reduce_scatter | solution.py:66
  126.7 5.8 collective-permute-done
  133.7 43.6 %all-gather.2.cloned.1.call-done = bf16[128,8192]{1,0:T(8,128)(2,1)} async-done(((bf16[128,1024]{1,0:T(8,128)(2,1)}), bf16[128,8192]{1,0:T(8,128)(2,1)}) %all-gather.2.cloned.1.call-update) | async-done | bytes 2097168 | tf_op jit(solution)/shard_map/while/body/eval_jaxpr/all_gather | solution.py:56
  191.4 6.1 convolution_convert_fusion.13
  197.5 41.7 %reduce-scatter.3.cloned.1.call-done = bf16[128,1024]{1,0:T(8,128)(2,1)} async-done(((bf16[128,8192]{1,0:T(8,128)(2,1)}), bf16[128,1024]{1,0:T(8,128)(2,1)}) %reduce-scatter.3.cloned.1.call-update) | async-done | bytes 262160 | tf_op jit(solution)/shard_map/while/body/eval_jaxpr/reduce_scatter | solution.py:66
  248.7 43.3 %all-gather.2.cloned.1.call-done = bf16[128,8192]{1,0:T(8,128)(2,1)} async-done(((bf16[128,1024]{1,0:T(8,128)(2,1)}), bf16[128,8192]{1,0:T(8,128)(2,1)}) %all-gather.2.cloned.1.call-update) | async-done | bytes 2097168 | tf_op jit(solution)/shard_map/while/body/eval_jaxpr/all_gather | solution.py:56
  306.1 6.1 convolution_convert_fusion.13
  312.2 41.6 %reduce-scatter.3.cloned.1.call-done = bf16[128,1024]{1,0:T(8,128)(2,1)} async-done(((bf16[128,8192]{1,0:T(8,128)(2,1)}), bf16[128,1024]{1,0:T(8,128)(2,1)}) %reduce-scatter.3.cloned.1.call-update) | async-done | bytes 262160 | tf_op jit(solution)/shard_map/while/body/eval_jaxpr/reduce_scatter | solution.py:66
  356.2 5.8 collective-permute-done
  363.3 43.6 %all-gather.2.cloned.1.call-done = bf16[128,8192]{1,0:T(8,128)(2,1)} async-done(((bf16[128,1024]{1,0:T(8,128)(2,1)}), bf16[128,8192]{1,0:T(8,128)(2,1)}) %all-gather.2.cloned.1.call-update) | async-done | bytes 2097168 | tf_op jit(solution)/shard_map/while/body/eval_jaxpr/all_gather | solution.py:56
  421.0 6.1 convolution_convert_fusion.13
  427.0 41.7 %reduce-scatter.3.cloned.1.call-done = bf16[128,1024]{1,0:T(8,128)(2,1)} async-done(((bf16[128,8192]{1,0:T(8,128)(2,1)}), bf16[128,1024]{1,0:T(8,128)(2,1)}) %reduce-scatter.3.cloned.1.call-update) | async-done | bytes 262160 | tf_op jit(solution)/shard_map/while/body/eval_jaxpr/reduce_scatter | solution.py:66
  480.6 11.3 %all-to-all-start.1 = ((bf16[4,2,64,128]{3,2,1,0:T(8,128)(2,1)}), bf16[4,2,64,128]{3,2,1,0:T(8,128)(2,1)S(1)}, u32[]{:S(2)}, u32[]{:S(2)}) async-start(bf16[4,2,64,128]{3,2,1,0:T(8,128)(2,1)} %copy.87), calls=%async_computation.3 | async-start | bytes 262144 | tf_op jit(solution)/shard_map/all_to_all | solution.py:200
  506.4 594.5 %while.48 = (s32[]{:T(128)}, bf16[8,1024]{1,0:T(8,128)(2,1)S(1)}, bf16[8,4,1,128]{3,0,2,1:T(8,128)(2,1)S(1)}, bf16[8,4,1,128]{3,0,2,1:T(8,128)(2,1)S(1)}, bf16[4...) while((s32[]{:T(128)}, bf16[8,1024]{1,0:T(8,128)(2,1)S(1)}, ...), condition=%wide.region_16.17_spmd.clone.clone, body=%wide.region_11.16_spmd.clone.clone.sunk | while | flops 170604480 | bytes 23151540 | solution.py:269
  506.7 21.8 %all_gather.26 = bf16[8,8192]{1,0:T(8,128)(2,1)S(1)} all-gather(bf16[8,1024]{1,0:T(8,128)(2,1)S(1)} %bitcast_select_fusion.3), channel_id=1, replica_groups=mesh['phase'=4,'grp'=4,'tp'=8] {'tp'}, dimensions={1}, use_global_device_ids=true | all-gather | bytes 147456 | tf_op jit(solution)/shard_map/while/body/eval_jaxpr/all_gather | solution.py:56
  543.9 35.6 %reduce-scatter.5.cloned.1.call-done = bf16[8,1024]{1,0:T(8,128)(2,1)} async-done(((bf16[8,8192]{1,0:T(8,128)(2,1)}), bf16[8,1024]{1,0:T(8,128)(2,1)}) %reduce-scatter.5.cloned.1.call-update) | async-done | bytes 16400 | tf_op jit(solution)/shard_map/while/body/eval_jaxpr/reduce_scatter | solution.py:66
  584.8 22.1 %all_gather.26 = bf16[8,8192]{1,0:T(8,128)(2,1)S(1)} all-gather(bf16[8,1024]{1,0:T(8,128)(2,1)S(1)} %bitcast_select_fusion.3), channel_id=1, replica_groups=mesh['phase'=4,'grp'=4,'tp'=8] {'tp'}, dimensions={1}, use_global_device_ids=true | all-gather | bytes 147456 | tf_op jit(solution)/shard_map/while/body/eval_jaxpr/all_gather | solution.py:56
  622.3 43.3 %reduce-scatter.5.cloned.1.call-done = bf16[8,1024]{1,0:T(8,128)(2,1)} async-done(((bf16[8,8192]{1,0:T(8,128)(2,1)}), bf16[8,1024]{1,0:T(8,128)(2,1)}) %reduce-scatter.5.cloned.1.call-update) | async-done | bytes 16400 | tf_op jit(solution)/shard_map/while/body/eval_jaxpr/reduce_scatter | solution.py:66
  671.0 21.9 %all_gather.26 = bf16[8,8192]{1,0:T(8,128)(2,1)S(1)} all-gather(bf16[8,1024]{1,0:T(8,128)(2,1)S(1)} %bitcast_select_fusion.3), channel_id=1, replica_groups=mesh['phase'=4,'grp'=4,'tp'=8] {'tp'}, dimensions={1}, use_global_device_ids=true | all-gather | bytes 147456 | tf_op jit(solution)/shard_map/while/body/eval_jaxpr/all_gather | solution.py:56
  708.2 43.2 %reduce-scatter.5.cloned.1.call-done = bf16[8,1024]{1,0:T(8,128)(2,1)} async-done(((bf16[8,8192]{1,0:T(8,128)(2,1)}), bf16[8,1024]{1,0:T(8,128)(2,1)}) %reduce-scatter.5.cloned.1.call-update) | async-done | bytes 16400 | tf_op jit(solution)/shard_map/while/body/eval_jaxpr/reduce_scatter | solution.py:66
  756.8 22.2 %all_gather.26 = bf16[8,8192]{1,0:T(8,128)(2,1)S(1)} all-gather(bf16[8,1024]{1,0:T(8,128)(2,1)S(1)} %bitcast_select_fusion.3), channel_id=1, replica_groups=mesh['phase'=4,'grp'=4,'tp'=8] {'tp'}, dimensions={1}, use_global_device_ids=true | all-gather | bytes 147456 | tf_op jit(solution)/shard_map/while/body/eval_jaxpr/all_gather | solution.py:56
  794.3 43.1 %reduce-scatter.5.cloned.1.call-done = bf16[8,1024]{1,0:T(8,128)(2,1)} async-done(((bf16[8,8192]{1,0:T(8,128)(2,1)}), bf16[8,1024]{1,0:T(8,128)(2,1)}) %reduce-scatter.5.cloned.1.call-update) | async-done | bytes 16400 | tf_op jit(solution)/shard_map/while/body/eval_jaxpr/reduce_scatter | solution.py:66
  842.8 22.1 %all_gather.26 = bf16[8,8192]{1,0:T(8,128)(2,1)S(1)} all-gather(bf16[8,1024]{1,0:T(8,128)(2,1)S(1)} %bitcast_select_fusion.3), channel_id=1, replica_groups=mesh['phase'=4,'grp'=4,'tp'=8] {'tp'}, dimensions={1}, use_global_device_ids=true | all-gather | bytes 147456 | tf_op jit(solution)/shard_map/while/body/eval_jaxpr/all_gather | solution.py:56
  880.4 43.4 %reduce-scatter.5.cloned.1.call-done = bf16[8,1024]{1,0:T(8,128)(2,1)} async-done(((bf16[8,8192]{1,0:T(8,128)(2,1)}), bf16[8,1024]{1,0:T(8,128)(2,1)}) %reduce-scatter.5.cloned.1.call-update) | async-done | bytes 16400 | tf_op jit(solution)/shard_map/while/body/eval_jaxpr/reduce_scatter | solution.py:66
  929.1 21.9 %all_gather.26 = bf16[8,8192]{1,0:T(8,128)(2,1)S(1)} all-gather(bf16[8,1024]{1,0:T(8,128)(2,1)S(1)} %bitcast_select_fusion.3), channel_id=1, replica_groups=mesh['phase'=4,'grp'=4,'tp'=8] {'tp'}, dimensions={1}, use_global_device_ids=true | all-gather | bytes 147456 | tf_op jit(solution)/shard_map/while/body/eval_jaxpr/all_gather | solution.py:56
  966.3 43.3 %reduce-scatter.5.cloned.1.call-done = bf16[8,1024]{1,0:T(8,128)(2,1)} async-done(((bf16[8,8192]{1,0:T(8,128)(2,1)}), bf16[8,1024]{1,0:T(8,128)(2,1)}) %reduce-scatter.5.cloned.1.call-update) | async-done | bytes 16400 | tf_op jit(solution)/shard_map/while/body/eval_jaxpr/reduce_scatter | solution.py:66
  1015.0 21.9 %all_gather.26 = bf16[8,8192]{1,0:T(8,128)(2,1)S(1)} all-gather(bf16[8,1024]{1,0:T(8,128)(2,1)S(1)} %bitcast_select_fusion.3), channel_id=1, replica_groups=mesh['phase'=4,'grp'=4,'tp'=8] {'tp'}, dimensions={1}, use_global_device_ids=true | all-gather | bytes 147456 | tf_op jit(solution)/shard_map/while/body/eval_jaxpr/all_gather | solution.py:56
  1052.3 43.3 %reduce-scatter.5.cloned.1.call-done = bf16[8,1024]{1,0:T(8,128)(2,1)} async-done(((bf16[8,8192]{1,0:T(8,128)(2,1)}), bf16[8,1024]{1,0:T(8,128)(2,1)}) %reduce-scatter.5.cloned.1.call-update) | async-done | bytes 16400 | tf_op jit(solution)/shard_map/while/body/eval_jaxpr/reduce_scatter | solution.py:66
  (428 shorter events, 253.7 us)
Async XLA Ops:
  9.7 470.9 %all-to-all-start = ((bf16[4,2,4,1024]{3,2,1,0:T(4,128)(2,1)}), bf16[4,2,4,1024]{3,2,1,0:T(4,128)(2,1)S(1)}, u32[]{:S(2)}, u32[]{:S(2)}) async-start(bf16[4,2,4,1024]{3,2,1,0:T(4,128)(2,1)} %copy.84), calls=%async_computation.2 | async-start | bytes 131072 | tf_op jit(solution)/shard_map/all_to_all | solution.py:202
  21.3 470.6 %copy-start.7 = (s32[4,4]{1,0:T(4,128)S(1)}, s32[4,4]{1,0:T(4,128)}, u32[]{:S(2)}) copy-start(s32[4,4]{1,0:T(4,128)} %param.14) | copy-start | bytes 196
  21.3 41.1 %all-gather.2.cloned.1.call-start = ((), (), s32[]{:S(2)}) async-start(), calls=%async_computation.5 | async-start | bytes 2359296 | tf_op jit(solution)/shard_map/while/body/eval_jaxpr/all_gather | solution.py:56
  22.1 102.1 %reduce-scatter.3.cloned.1.call-start = ((), (), s32[]{:S(2)}) async-start(), calls=%async_computation.6 | async-start | bytes 2359296 | tf_op jit(solution)/shard_map/while/body/eval_jaxpr/reduce_scatter | solution.py:66
  125.4 7.1 collective-permute-start
  132.5 44.9 %all-gather.2.cloned.1.call-start = ((), (), s32[]{:S(2)}) async-start(), calls=%async_computation.5 | async-start | bytes 2359296 | tf_op jit(solution)/shard_map/while/body/eval_jaxpr/all_gather | solution.py:56
  133.2 49.8 %copy-start.4 = (f32[1,8192]{1,0:T(1,128)S(1)}, f32[1,8192]{1,0:T(1,128)}, u32[]{:S(2)}) copy-start(f32[1,8192]{1,0:T(1,128)} %get-tuple-element.1399) | copy-start | bytes 98308 | tf_op jit(solution)/shard_map/while
  133.2 106.0 %reduce-scatter.3.cloned.1.call-start = ((), (), s32[]{:S(2)}) async-start(), calls=%async_computation.6 | async-start | bytes 2359296 | tf_op jit(solution)/shard_map/while/body/eval_jaxpr/reduce_scatter | solution.py:66
  240.3 7.1 collective-permute-start
  247.4 44.5 %all-gather.2.cloned.1.call-start = ((), (), s32[]{:S(2)}) async-start(), calls=%async_computation.5 | async-start | bytes 2359296 | tf_op jit(solution)/shard_map/while/body/eval_jaxpr/all_gather | solution.py:56
  248.2 105.6 %reduce-scatter.3.cloned.1.call-start = ((), (), s32[]{:S(2)}) async-start(), calls=%async_computation.6 | async-start | bytes 2359296 | tf_op jit(solution)/shard_map/while/body/eval_jaxpr/reduce_scatter | solution.py:66
  354.9 7.1 collective-permute-start
  362.0 44.9 %all-gather.2.cloned.1.call-start = ((), (), s32[]{:S(2)}) async-start(), calls=%async_computation.5 | async-start | bytes 2359296 | tf_op jit(solution)/shard_map/while/body/eval_jaxpr/all_gather | solution.py:56
  362.8 49.8 %copy-start.4 = (f32[1,8192]{1,0:T(1,128)S(1)}, f32[1,8192]{1,0:T(1,128)}, u32[]{:S(2)}) copy-start(f32[1,8192]{1,0:T(1,128)} %get-tuple-element.1399) | copy-start | bytes 98308 | tf_op jit(solution)/shard_map/while
  362.8 106.0 %reduce-scatter.3.cloned.1.call-start = ((), (), s32[]{:S(2)}) async-start(), calls=%async_computation.6 | async-start | bytes 2359296 | tf_op jit(solution)/shard_map/while/body/eval_jaxpr/reduce_scatter | solution.py:66
  469.9 7.1 collective-permute-start
  480.6 16.4 %all-to-all-start.1 = ((bf16[4,2,64,128]{3,2,1,0:T(8,128)(2,1)}), bf16[4,2,64,128]{3,2,1,0:T(8,128)(2,1)S(1)}, u32[]{:S(2)}, u32[]{:S(2)}) async-start(bf16[4,2,64,128]{3,2,1,0:T(8,128)(2,1)} %copy.87), calls=%async_computation.3 | async-start | bytes 262144 | tf_op jit(solution)/shard_map/all_to_all | solution.py:200
  497.0 9.4 all-to-all-start.2
  506.5 73.0 %reduce-scatter.5.cloned.1.call-start = ((), (), s32[]{:S(2)}) async-start(), calls=%async_computation.7 | async-start | bytes 147456 | tf_op jit(solution)/shard_map/while/body/eval_jaxpr/reduce_scatter | solution.py:66
  580.1 4.5 collective-permute-start.1
  584.6 81.0 %reduce-scatter.5.cloned.1.call-start = ((), (), s32[]{:S(2)}) async-start(), calls=%async_computation.7 | async-start | bytes 147456 | tf_op jit(solution)/shard_map/while/body/eval_jaxpr/reduce_scatter | solution.py:66
  666.3 4.5 collective-permute-start.1
  670.8 80.6 %reduce-scatter.5.cloned.1.call-start = ((), (), s32[]{:S(2)}) async-start(), calls=%async_computation.7 | async-start | bytes 147456 | tf_op jit(solution)/shard_map/while/body/eval_jaxpr/reduce_scatter | solution.py:66
  752.2 4.5 collective-permute-start.1
  756.6 80.8 %reduce-scatter.5.cloned.1.call-start = ((), (), s32[]{:S(2)}) async-start(), calls=%async_computation.7 | async-start | bytes 147456 | tf_op jit(solution)/shard_map/while/body/eval_jaxpr/reduce_scatter | solution.py:66
  838.2 4.5 collective-permute-start.1
  842.7 81.0 %reduce-scatter.5.cloned.1.call-start = ((), (), s32[]{:S(2)}) async-start(), calls=%async_computation.7 | async-start | bytes 147456 | tf_op jit(solution)/shard_map/while/body/eval_jaxpr/reduce_scatter | solution.py:66
  924.5 4.5 collective-permute-start.1
  928.9 80.7 %reduce-scatter.5.cloned.1.call-start = ((), (), s32[]{:S(2)}) async-start(), calls=%async_computation.7 | async-start | bytes 147456 | tf_op jit(solution)/shard_map/while/body/eval_jaxpr/reduce_scatter | solution.py:66
  1010.4 4.5 collective-permute-start.1
  1014.9 80.8 %reduce-scatter.5.cloned.1.call-start = ((), (), s32[]{:S(2)}) async-start(), calls=%async_computation.7 | async-start | bytes 147456 | tf_op jit(solution)/shard_map/while/body/eval_jaxpr/reduce_scatter | solution.py:66
  1096.4 4.5 collective-permute-start.1
  (23 other events, 548.4 us)
Sparse Core Ops, SparseCore 0:
  24.3 37.9 all-gather.1
  82.7 41.5 reduce-scatter.2
  135.5 41.7 all-gather.1
  197.6 41.5 reduce-scatter.2
  250.2 41.7 all-gather.1
  312.3 41.4 reduce-scatter.2
  365.1 41.7 all-gather.1
  427.2 41.5 reduce-scatter.2
  544.0 35.3 reduce-scatter.4
  622.4 43.1 reduce-scatter.4
  708.4 43.0 reduce-scatter.4
  794.5 42.9 reduce-scatter.4
  880.5 43.2 reduce-scatter.4
  966.5 43.1 reduce-scatter.4
  1052.5 43.1 reduce-scatter.4
where the time goes:
time: 1120 us; the launch traced here: 1110 us
  waiting for transfers between devices  687 us (61%)
  matrix products  170 us (15%)
  blocking collectives  154 us (14%)
  other arithmetic  36.4 us (3%)
  starting transfers between devices  35.9 us (3%)
  between operations  13.9 us (1%)
    reduce_scatter x11, waiting for transfers between devices, project_out(): lax.psum_scatter(partial_sum.astype(jnp.bfloat16), 'tp', scatter_dimensio...  462 us
    all_gather x4, waiting for transfers between devices, project_in(): whole_rows = lax.all_gather(entering, 'tp', axis=1, tiled=True)  170 us
    all_gather x7, blocking collectives, project_in(): whole_rows = lax.all_gather(entering, 'tp', axis=1, tiled=True)  154 us
    dot_general x11, matrix products, project_out(): partial_sum = jnp.dot(head_out, out_w, preferred_element_type=jnp.float32)  60.9 us
    dot_general x11, matrix products, project_in(): queries = jnp.dot(normal_rows, query_w, preferred_element_type=jnp.float32)  52 us
    ppermute x11, waiting for transfers between devices, shifted(): lax.ppermute(value, axis, [(source, source + steps) for source in range(i...  45.3 us
    dot_general x11, matrix products, project_in(): new_keys = jnp.dot(normal_rows, key_w, preferred_element_type=jnp.float32)  26.5 us
    dot_general x11, matrix products, project_in(): jnp.dot(normal_rows, value_w, preferred_element_type=jnp.float32)  24 us
  transfers between devices with their start and end apart: 29, of which 28 were waited for; matrix products, arithmetic and copies ran while one was open for 9% of the time, Pallas kernels for 0%

commit v1 on v0

v1 whole, which is shorter than its diff:
```python
import functools
import math

import jax
import jax.numpy as jnp
from jax import lax
from jax.experimental import pallas as pl
from jax.experimental.pallas import tpu as pltpu
from jax.sharding import PartitionSpec as P

D = 8192
HQ = 4
HD = 128
STEPS = 4
DOCS = 4
CAP = 2
N_TP = 8
N_GRP = 4
N_PHASE = 4
PTOK = 128
ROWS = PTOK + STEPS * DOCS
CH = D // N_TP
NQKV = (HQ + 2) * HD
KEYS = 256
EPS = 1e-06
THETA = 1000000.0
MESH = pl.DeviceIdType.MESH

SIZES = (32, 32, 32, 32, 16)
STARTS = tuple(sum(SIZES[:i]) for i in range(len(SIZES)))
NB = len(SIZES)
RMAX = max(SIZES)


def kernel(
    lens_ref, dest_ref, x_ref, steps_ref, gain_ref, wq_hbm, wk_hbm, wv_hbm, wo_hbm,
    pre_out, dec_out,
    w, wo, xg, rs, st, xo, own, acc, ssq, hb, kb, vb, cosb, sinb, bias, dsend, drecv,
    wsem, first_send, ag_send, ag_recv, rs_send, rs_recv, dec_send, dec_recv,
):
    phase = lax.axis_index("phase")
    grp = lax.axis_index("grp")
    me = lax.axis_index("tp")
    my_y, my_z = me % 4, me // 4

    def peer(k):
        return ((my_z + k // 4) % 2) * 4 + (my_y + k % 4) % 4

    def weight_copies(c):
        rows = pl.ds(c * CH, CH)
        return (
            pltpu.make_async_copy(wq_hbm.at[rows], w.at[rows, pl.ds(0, HQ * HD)], wsem.at[0, c]),
            pltpu.make_async_copy(wk_hbm.at[rows], w.at[rows, pl.ds(HQ * HD, HD)], wsem.at[1, c]),
            pltpu.make_async_copy(wv_hbm.at[rows], w.at[rows, pl.ds(HQ * HD + HD, HD)], wsem.at[2, c]),
        )

    def out_weight_copy(c):
        cols = pl.ds(pl.multiple_of(c * CH, CH), CH)
        return pltpu.make_async_copy(wo_hbm.at[:, cols], wo.at[:, cols], wsem.at[3, c])

    @pl.loop(0, N_TP)
    def _(k):
        for copy in weight_copies(peer(k)):
            copy.start()

    @pl.loop(0, N_TP)
    def _(k):
        out_weight_copy(peer(N_TP - 1 - k)).start()

    barrier = pltpu.get_barrier_semaphore()

    def greet(device):
        pl.semaphore_signal(barrier, inc=1, device_id=device, device_id_type=MESH)

    for k in range(1, N_TP):
        greet((phase, grp, peer(k)))
    for k in range(1, N_GRP):
        greet((phase, (grp + k) % N_GRP, me))

    @pl.when(phase > 0)
    def _():
        for k in range(N_TP):
            greet((phase - 1, grp, peer(k)))

    @pl.when(phase < N_PHASE - 1)
    def _():
        for k in range(N_TP):
            greet((phase + 1, grp, peer(k)))

    lens = [lens_ref[grp, d] for d in range(DOCS)]
    starts = [jnp.int32(0)]
    for d in range(DOCS):
        starts.append(starts[-1] + lens[d])

    def pick(values, index):
        out = jnp.full(index.shape, values[-1], jnp.int32)
        for d in range(DOCS - 1):
            out = jnp.where(index == d, values[d], out)
        return out

    def segment_and_place(row):
        of_prompt = sum((row >= starts[d]).astype(jnp.int32) for d in range(1, DOCS))
        of_step = (row - PTOK) & (DOCS - 1)
        step = (row - PTOK) >> 2
        segment = jnp.where(row < PTOK, of_prompt, of_step)
        place = jnp.where(row < PTOK, row - pick(starts[:DOCS], of_prompt), pick(lens, of_step) + step)
        return jnp.where(row < ROWS, segment, -1), place

    seg_q, place_q = segment_and_place(lax.broadcasted_iota(jnp.int32, (ROWS, HD), 0))
    lane = lax.broadcasted_iota(jnp.int32, (ROWS, HD), 1)
    half = (lane & (HD // 2 - 1)).astype(jnp.float32)
    angle = place_q.astype(jnp.float32) * jnp.exp(half * (-2.0 / HD * math.log(THETA)))
    cosb[...] = jnp.cos(angle)
    sine = jnp.sin(angle)
    sinb[...] = jnp.where(lane < HD // 2, -sine, sine)
    for part in range(KEYS // HD):
        seg_k, place_k = segment_and_place(lax.broadcasted_iota(jnp.int32, (ROWS, HD), 1) + part * HD)
        bias[:, part * HD : (part + 1) * HD] = jnp.where((seg_q == seg_k) & (place_k <= place_q), 0.0, -1e30)
    kb[...] = jnp.zeros_like(kb)
    vb[...] = jnp.zeros_like(vb)

    @pl.when(phase == 0)
    def _():
        xg[me, 0:PTOK] = x_ref[...]
        xg[me, PTOK:ROWS] = steps_ref[...]

    middle = ((phase > 0) & (phase < N_PHASE - 1)).astype(jnp.int32)
    pl.semaphore_wait(barrier, N_TP - 1 + N_GRP - 1 + N_TP + N_TP * middle)

    def first_copy(b, k):
        rows = pl.ds(STARTS[b], SIZES[b])
        return pltpu.make_async_remote_copy(
            src_ref=xg.at[me, rows], dst_ref=xg.at[me, rows],
            send_sem=first_send.at[b, k], recv_sem=ag_recv.at[b, me],
            device_id=(0, grp, peer(N_TP - k)), device_id_type=MESH)

    def next_copy(b, k):
        rows = pl.ds(STARTS[b], SIZES[b])
        return pltpu.make_async_remote_copy(
            src_ref=xo.at[rows], dst_ref=xg.at[me, rows],
            send_sem=ag_send.at[b, k], recv_sem=ag_recv.at[b, me],
            device_id=(phase + 1, grp, peer(k)), device_id_type=MESH)

    def part_copy(b, k):
        rows = pl.ds(STARTS[b], SIZES[b])
        return pltpu.make_async_remote_copy(
            src_ref=st.at[k, rows], dst_ref=rs.at[me, rows],
            send_sem=rs_send.at[b, k], recv_sem=rs_recv.at[b, me],
            device_id=(phase, grp, peer(k)), device_id_type=MESH)

    def arrival(buffer, sems, b, c):
        rows = pl.ds(STARTS[b], SIZES[b])
        return pltpu.make_async_remote_copy(
            src_ref=buffer.at[c, rows], dst_ref=buffer.at[c, rows],
            send_sem=rs_send.at[b, 0], recv_sem=sems.at[b, c],
            device_id=(phase, grp, peer(1)), device_id_type=MESH)

    def first_sends(b):
        if b < NB:
            @pl.when(phase == 0)
            def _():
                for k in range(1, N_TP):
                    first_copy(b, k).start()

    def project_in(b):
        first, size = STARTS[b], SIZES[b]
        acc[0:size] = jnp.zeros((size, NQKV), jnp.float32)
        ssq[0:size] = jnp.zeros((size, HD), jnp.float32)

        @pl.loop(0, N_TP)
        def _(k):
            c = peer(k)

            @pl.when((phase > 0) | (k > 0))
            def _():
                arrival(xg, ag_recv, b, c).wait_recv()

            if b == 0:
                for copy in weight_copies(c):
                    copy.wait()
            values = xg[c, first : first + size, :].astype(jnp.float32)
            squares = values * values
            ssq[0:size] += sum(squares[:, i * HD : (i + 1) * HD] for i in range(CH // HD))
            scaled = (values * gain_ref[:, pl.ds(pl.multiple_of(c * CH, CH), CH)]).astype(jnp.bfloat16)
            acc[0:size] += jnp.dot(scaled, w[pl.ds(c * CH, CH), :], preferred_element_type=jnp.float32)

    def attend(b):
        first, size = STARTS[b], SIZES[b]
        rows = slice(first, first + size)
        factor = lax.rsqrt(jnp.sum(ssq[0:size], axis=-1, keepdims=True) * (1.0 / D) + EPS)
        cosine, sine = cosb[rows], sinb[rows]

        def rotated(values):
            return (values * cosine + pltpu.roll(values, HD // 2, 1) * sine).astype(jnp.bfloat16)

        projected = acc[0:size] * factor
        heads = [rotated(projected[:, h * HD : (h + 1) * HD]) for h in range(HQ + 1)]
        kb[rows] = heads[HQ]
        vb[rows] = projected[:, (HQ + 1) * HD :].astype(jnp.bfloat16)
        n_keys = HD if first + size <= HD else KEYS
        queries = jnp.concatenate(heads[:HQ], axis=0)
        scores = lax.dot_general(
            queries, kb[0:n_keys], (((1,), (1,)), ((), ())), preferred_element_type=jnp.float32)
        mask = bias[rows, 0:n_keys]
        scores = scores * (1.0 / math.sqrt(HD)) + jnp.concatenate([mask] * HQ, axis=0)
        raised = jnp.exp(scores - jnp.max(scores, axis=-1, keepdims=True))
        probability = (raised / jnp.sum(raised, axis=-1, keepdims=True)).astype(jnp.bfloat16)
        mixed = jnp.dot(probability, vb[0:n_keys], preferred_element_type=jnp.float32).astype(jnp.bfloat16)
        for h in range(HQ):
            hb[0:size, h * HD : (h + 1) * HD] = mixed[h * size : (h + 1) * size]

    def project_out(b):
        first, size = STARTS[b], SIZES[b]

        def product(k):
            c = peer(k)
            if b == 0:
                out_weight_copy(c).wait()
            cols = pl.ds(pl.multiple_of(c * CH, CH), CH)
            return jnp.dot(hb[0:size], wo[:, cols], preferred_element_type=jnp.float32)

        @pl.loop(0, N_TP - 1)
        def _(j):
            k = N_TP - 1 - j
            st[k, first : first + size] = product(k).astype(jnp.bfloat16)
            part_copy(b, k).start()

        own[0:size] = product(0)

    def finish(b):
        first, size = STARTS[b], SIZES[b]
        rows = slice(first, first + size)
        own[0:size] += xg[me, rows].astype(jnp.float32)

        @pl.loop(1, N_TP)
        def _(k):
            c = peer(k)
            arrival(rs, rs_recv, b, c).wait_recv()
            own[0:size] += rs[c, rows].astype(jnp.float32)

        result = own[0:size].astype(jnp.bfloat16)
        xo[rows] = result

        @pl.when(phase < N_PHASE - 1)
        def _():
            for k in range(N_TP - 1, -1, -1):
                next_copy(b, k).start()

        inside = min(first + size, PTOK) - first
        if inside > 0:
            pre_out[first : first + inside] = result[0:inside]

    first_sends(0)
    for b in range(NB):
        first_sends(b + 1)
        project_in(b)
        attend(b)
        project_out(b)
        finish(b)

    row = lax.broadcasted_iota(jnp.int32, (N_GRP * STEPS * CAP, STEPS * DOCS), 0)
    col = lax.broadcasted_iota(jnp.int32, (N_GRP * STEPS * CAP, STEPS * DOCS), 1)
    dests = [dest_ref[grp, d] for d in range(DOCS)]
    ranks = [
        sum([(dests[e] == dests[d]).astype(jnp.int32) for e in range(d)], jnp.int32(0)) for d in range(DOCS)
    ]
    doc = col & (DOCS - 1)
    chosen = (
        (pick(dests, doc) == (row >> 3)) & (pick(ranks, doc) == (row & 1)) & ((col >> 2) == ((row >> 1) & 3))
    )
    chosen = jnp.where(chosen, 1.0, 0.0).astype(jnp.bfloat16)
    picked = jnp.dot(chosen, xo[PTOK:ROWS], preferred_element_type=jnp.float32)
    dsend[...] = picked.reshape(N_GRP, STEPS * CAP, CH)
    drecv[grp] = dsend[grp]

    def decode_copy(k):
        to = (grp + k) % N_GRP
        return pltpu.make_async_remote_copy(
            src_ref=dsend.at[to], dst_ref=drecv.at[grp],
            send_sem=dec_send.at[k], recv_sem=dec_recv.at[k],
            device_id=(phase, to, me), device_id_type=MESH)

    for k in range(1, N_GRP):
        decode_copy(k).start()

    @pl.when(phase == 0)
    def _():
        for b in range(NB):
            for k in range(1, N_TP):
                first_copy(b, k).wait_send()

    @pl.when(phase < N_PHASE - 1)
    def _():
        for b in range(NB):
            for k in range(N_TP):
                next_copy(b, k).wait_send()

    for b in range(NB):
        for k in range(1, N_TP):
            part_copy(b, k).wait_send()

    for k in range(1, N_GRP):
        came = (grp + N_GRP - k) % N_GRP
        pltpu.make_async_remote_copy(
            src_ref=dsend.at[came], dst_ref=drecv.at[came],
            send_sem=dec_send.at[k], recv_sem=dec_recv.at[k],
            device_id=(phase, came, me), device_id_type=MESH).wait_recv()
        decode_copy(k).wait_send()
    n = N_GRP * STEPS * CAP
    row = lax.broadcasted_iota(jnp.int32, (n, n), 0)
    col = lax.broadcasted_iota(jnp.int32, (n, n), 1)
    wanted = ((row >> 1) & 3) * 8 + (row >> 3) * 2 + (row & 1)
    order = jnp.where(col == wanted, 1.0, 0.0).astype(jnp.bfloat16)
    arranged = jnp.dot(
        order, drecv[...].reshape(n, CH).astype(jnp.bfloat16), preferred_element_type=jnp.float32)
    dec_out[...] = arranged.reshape(STEPS, N_GRP * CAP, CH).astype(jnp.bfloat16)


def body(
    prompt_embed, prompt_lengths, decode_group, step_embed, norm_gain, w_query, w_key, w_value, w_out,
):
    smem = pl.BlockSpec(memory_space=pltpu.SMEM)
    vmem = pl.BlockSpec(memory_space=pltpu.VMEM)
    hbm = pl.BlockSpec(memory_space=pl.ANY)
    bf16, f32 = jnp.bfloat16, jnp.float32
    dma = pltpu.SemaphoreType.DMA
    prefill, decode = pl.pallas_call(
        kernel,
        name="layers",
        out_shape=(
            jax.ShapeDtypeStruct((PTOK, CH), bf16),
            jax.ShapeDtypeStruct((STEPS, N_GRP * CAP, CH), bf16),
        ),
        in_specs=[smem, smem, vmem, vmem, vmem, hbm, hbm, hbm, hbm],
        out_specs=(vmem, vmem),
        scratch_shapes=[
            pltpu.VMEM((D, NQKV), bf16),
            pltpu.VMEM((HQ * HD, D), bf16),
            pltpu.VMEM((N_TP, ROWS, CH), bf16),
            pltpu.VMEM((N_TP, ROWS, CH), bf16),
            pltpu.VMEM((N_TP, ROWS, CH), bf16),
            pltpu.VMEM((ROWS, CH), bf16),
            pltpu.VMEM((RMAX, CH), f32),
            pltpu.VMEM((RMAX, NQKV), f32),
            pltpu.VMEM((RMAX, HD), f32),
            pltpu.VMEM((RMAX, HQ * HD), bf16),
            pltpu.VMEM((KEYS, HD), bf16),
            pltpu.VMEM((KEYS, HD), bf16),
            pltpu.VMEM((ROWS, HD), f32),
            pltpu.VMEM((ROWS, HD), f32),
            pltpu.VMEM((ROWS, KEYS), f32),
            pltpu.VMEM((N_GRP, STEPS * CAP, CH), f32),
            pltpu.VMEM((N_GRP, STEPS * CAP, CH), f32),
            dma((4, N_TP)),
            dma((NB, N_TP)),
            dma((NB, N_TP)),
            dma((NB, N_TP)),
            dma((NB, N_TP)),
            dma((NB, N_TP)),
            dma((N_GRP,)),
            dma((N_GRP,)),
        ],
        compiler_params=pltpu.CompilerParams(
            collective_id=0, has_side_effects=True, vmem_limit_bytes=48 << 20),
    )(
        prompt_lengths,
        decode_group.reshape(N_GRP, DOCS),
        prompt_embed,
        step_embed.reshape(STEPS * DOCS, CH),
        norm_gain,
        w_query[0],
        w_key[0],
        w_value[0],
        w_out[0],
    )
    return prefill[None], decode[None]


def solution(mesh):
    return jax.shard_map(
        body,
        mesh=mesh,
        in_specs=(
            P("grp", "tp"),
            P(),
            P(),
            P(None, "grp", "tp"),
            P("phase", None),
            P("phase", None, "tp"),
            P("phase", None, "tp"),
            P("phase", None, "tp"),
            P("phase", "tp", None),
        ),
        out_specs=(P("phase", "grp", "tp"), P("phase", None, "grp", "tp")),
        check_vma=False,
    )
```

time: 1120 us -> 191 us (0.17); the launches traced: 1110 us -> 190 us
  waiting for transfers between devices: 687 us -> 0 us
  Pallas kernels: 0 us -> 181 us
  matrix products: 170 us -> 0 us
  blocking collectives: 154 us -> 0 us
  other arithmetic: 36.4 us -> 0 us
  starting transfers between devices: 35.9 us -> 0 us
  between operations: 13.9 us -> 0.65 us
    reduce_scatter x11 -> x0, waiting for transfers between devices: 462 us -> none  [project_out(): lax.psum_scatter(partial_sum.astype(jnp.bfloat16), 'tp', scatter_dimensio...]
    pallas_call x0 -> x1, Pallas kernels: none -> 181 us  [body(): pl.pallas_call(kernel, name='layers', out_shape=(jax.ShapeDtypeStruct((PT...]
    all_gather x4 -> x0, waiting for transfers between devices: 170 us -> none  [project_in(): whole_rows = lax.all_gather(entering, 'tp', axis=1, tiled=True)]
    dot_general x62 -> x0, matrix products: 168 us -> none  [the longest x11 60.9 us: project_out(): partial_sum = jnp.dot(head_out, out_w, preferred_element_type=jnp.float32)]
    all_gather x7 -> x0, blocking collectives: 154 us -> none  [project_in(): whole_rows = lax.all_gather(entering, 'tp', axis=1, tiled=True)]
    ppermute x11 -> x0, waiting for transfers between devices: 45.3 us -> none  [shifted(): lax.ppermute(value, axis, [(source, source + steps) for source in range(i...]
    all_to_all x3 -> x0, starting transfers between devices: 21.4 us -> none  [the longest x1 11.3 us: body(): lax.all_to_all(send_keys, 'grp', split_axis=0, concat_axis=0, tiled=True)]
    ppermute x11 -> x0, starting transfers between devices: 14.2 us -> none  [shifted(): lax.ppermute(value, axis, [(source, source + steps) for source in range(i...]
  transfers between devices with their start and end apart: 29 -> 0, of which waited for: 28 -> 0; matrix products, arithmetic and copies ran while one was open for 9% -> 0% of each run, Pallas kernels for 0% -> 0%
where the time goes in v1:
time: 191 us; the launch traced here: 190 us
  Pallas kernels  181 us (95%)
  local copies, waits for them, and re-layouts  8.35 us (4%)
    pallas_call x1, Pallas kernels, body(): pl.pallas_call(kernel, name='layers', out_shape=(jax.ShapeDtypeStruct((PT...  181 us
    unnamed x14, local copies, waits for them, and re-layouts  7.58 us

profile of v1, /device:TPU:7, one launch (start us, length us, event | category | flops | bytes accessed | tf_op | source)
XLA Modules:
  0.0 190.5 jit_solution(10324696852967339447)
XLA Ops:
  0.6 0.8 reshape.11.steps_ref
  1.4 0.0 copy-start
  1.4 1.6 copy-done
  3.0 0.0 copy-start.1
  3.0 1.6 copy-done.1
  4.6 0.0 copy-start.2
  4.6 0.9 copy-done.2
  5.5 0.0 copy-start.3
  5.5 0.8 copy-done.3
  6.3 0.0 copy-start.4
  6.3 0.7 copy-done.4
  7.0 0.0 copy-start.5
  7.0 0.7 copy-done.5
  7.7 181.5 %layers.1 = (bf16[128,1024]{1,0:T(8,128)(2,1)S(1)}, bf16[4,8,1024]{2,1,0:T(8,128)(2,1)S(1)}) custom-call(s32[4,4]{1,0:T(4,128)S(1)} %copy-done.4, s32[4,4]{1,0:T(4,128)S(1)} %bitcast.11, bf16[128,1024]{1,0:T(8,128)(2,1)S(1)} %copy-done.2, bf16[16,1024]{1,0:T(8,128)(2,1)S(1)} %reshape.11.steps_ref, f32[1,8192]{1,0:T(1,128)S(1)} %copy-done.3, ...), custom_call_target="tpu_custom_call" | custom-call | tf_op jit(solution)/shard_map/layers/pallas_call | solution.py:327
  189.2 0.7 copy.13
  189.9 0.6 copy.14
Async XLA Ops:
  1.4 1.6 copy-start
  3.0 1.6 copy-start.1
  4.6 0.9 copy-start.2
  5.5 0.8 copy-start.3
  6.3 0.7 copy-start.4
  7.0 0.7 copy-start.5

commit v2 on v1

v2 whole, which is shorter than its diff:
```python
import functools
import math

import jax
import jax.numpy as jnp
from jax import lax
from jax.experimental import pallas as pl
from jax.experimental.pallas import tpu as pltpu
from jax.sharding import PartitionSpec as P

D = 8192
HQ = 4
HD = 128
STEPS = 4
DOCS = 4
CAP = 2
N_TP = 8
N_GRP = 4
N_PHASE = 4
PTOK = 128
ROWS = PTOK + STEPS * DOCS
CH = D // N_TP
NQKV = (HQ + 2) * HD
KEYS = 256
EPS = 1e-06
THETA = 1000000.0
MESH = pl.DeviceIdType.MESH

R = 16
NB = ROWS // R
SLOTS = N_TP - 1
PASS_ON_AT = 2
FINISH_AT = 7
SLOT_FROM = ((0, 0), (1, 2), (0, 1), (1, 3), (0, 3), (1, 1), (1, 0), (0, 2))
NEIGHBOURS = ((0, 3), (0, 1), (1, 0))


def kernel(
    lens_hbm, dest_hbm, x_hbm, steps_hbm, gain_hbm, wq_hbm, wk_hbm, wv_hbm, wo_hbm,
    pre_out, dec_out,
    lens_ref, dest_ref, steps_ref, gain_ref, w, wo, xg, rs, st, xo, own, choice, kb, vb, cosb, sinb, bias,
    dsend, drecv,
    small_sem, wsem, first_send, next_send, hand_recv, ag_send, ag_recv, rs_send, rs_recv, dec_send, dec_recv,
):
    phase = lax.axis_index("phase")
    grp = lax.axis_index("grp")
    me = lax.axis_index("tp")
    my_y, my_z = me % 4, me // 4

    def at(row, along):
        return ((my_z + row) % 2) * 4 + (my_y + along) % 4

    def target(m):
        return at(1 - m // 4, 7 - m)

    opposite = at(1, 2)

    def slot(m, count=1):
        return pl.ds(m * CH, count * CH)

    def weight_copies(m):
        came = at(*SLOT_FROM[m])
        rows = pl.ds(came * CH, CH)
        return (
            pltpu.make_async_copy(wq_hbm.at[rows], w.at[slot(m), pl.ds(0, HQ * HD)], wsem.at[0, m]),
            pltpu.make_async_copy(wk_hbm.at[rows], w.at[slot(m), pl.ds(HQ * HD, HD)], wsem.at[1, m]),
            pltpu.make_async_copy(wv_hbm.at[rows], w.at[slot(m), pl.ds(HQ * HD + HD, HD)], wsem.at[2, m]),
            pltpu.make_async_copy(
                gain_hbm.at[:, pl.ds(pl.multiple_of(came * CH, CH), CH)], gain_ref.at[:, slot(m)], wsem.at[4, m]),
        )

    def out_weight_copy(m):
        cols = pl.ds(pl.multiple_of(target(m) * CH, CH), CH)
        return pltpu.make_async_copy(wo_hbm.at[:, cols], wo.at[:, slot(m)], wsem.at[3, m])

    barrier = pltpu.get_barrier_semaphore()

    def greet(device):
        pl.semaphore_signal(barrier, inc=1, device_id=device, device_id_type=MESH)

    for m in range(SLOTS):
        greet((phase, grp, target(m)))
    for k in range(1, N_GRP):
        greet((phase, (grp + k) % N_GRP, me))

    @pl.when(phase > 0)
    def _():
        greet((phase - 1, grp, me))
        greet((phase - 1, grp, opposite))

    @pl.when(phase < N_PHASE - 1)
    def _():
        greet((phase + 1, grp, me))
        greet((phase + 1, grp, opposite))

    small = [
        pltpu.make_async_copy(src, dst, small_sem.at[i])
        for i, (src, dst) in enumerate(((lens_hbm, lens_ref), (dest_hbm, dest_ref), (steps_hbm, steps_ref)))
    ]
    own_rows = pltpu.make_async_copy(x_hbm, xg.at[pl.ds(0, PTOK), slot(0)], small_sem.at[3])

    @pl.when(phase == 0)
    def _():
        own_rows.start()

    for copy in small:
        copy.start()
    for m in range(N_TP):
        for copy in weight_copies(m):
            copy.start()
    for m in range(N_TP):
        out_weight_copy(m).start()

    ahead = 1 + (phase == 0).astype(jnp.int32)

    def block(b):
        return pl.ds(pl.multiple_of(b * R, R), R)

    def first_copy(b):
        return pltpu.make_async_remote_copy(
            src_ref=xg.at[block(b), slot(0)], dst_ref=xg.at[block(b), slot(1)],
            send_sem=first_send, recv_sem=hand_recv.at[b, 1],
            device_id=(0, grp, opposite), device_id_type=MESH)

    def first_direct(m):
        row, along = SLOT_FROM[m]
        return pltpu.make_async_remote_copy(
            src_ref=xg.at[block(0), slot(0)], dst_ref=xg.at[block(0), slot(m)],
            send_sem=first_send, recv_sem=hand_recv.at[0, 1] if m == 1 else ag_recv.at[0, m // 2 - 1],
            device_id=(0, grp, at(row, 4 - along)), device_id_type=MESH)

    def next_copy(b, m):
        return pltpu.make_async_remote_copy(
            src_ref=xo.at[block(b)], dst_ref=xg.at[block(b), slot(m)],
            send_sem=next_send, recv_sem=hand_recv.at[b, m],
            device_id=(phase + 1, grp, (me, opposite)[m]), device_id_type=MESH)

    def forward_copy(b, n):
        return pltpu.make_async_remote_copy(
            src_ref=xg.at[block(b), slot(0, 2)], dst_ref=xg.at[block(b), slot(2 * n + 2, 2)],
            send_sem=ag_send, recv_sem=ag_recv.at[b, n],
            device_id=(phase, grp, at(*NEIGHBOURS[n])), device_id_type=MESH)

    def part_copy(b, m):
        return pltpu.make_async_remote_copy(
            src_ref=st.at[m, block(b)], dst_ref=rs.at[m, block(b)],
            send_sem=rs_send, recv_sem=rs_recv.at[b],
            device_id=(phase, grp, target(m)), device_id_type=MESH)

    def waiter(buffer, send_sem, recv_sem):
        return pltpu.make_async_remote_copy(
            src_ref=buffer, dst_ref=buffer, send_sem=send_sem, recv_sem=recv_sem,
            device_id=(phase, grp, target(0)), device_id_type=MESH)

    def forward(b):
        pl.when(phase > 0)(waiter(xg.at[block(b), slot(0)], rs_send, hand_recv.at[b, 0]).wait_recv)
        waiter(xg.at[block(b), slot(1)], rs_send, hand_recv.at[b, 1]).wait_recv()

        @pl.when((phase > 0) | (b > 0))
        def _():
            for n in range(len(NEIGHBOURS)):
                forward_copy(b, n).start()

    middle = ((phase > 0) & (phase < N_PHASE - 1)).astype(jnp.int32)
    pl.semaphore_wait(barrier, SLOTS + N_GRP - 1 + 2 + 2 * middle)
    for copy in small:
        copy.wait()

    @pl.when(phase == 0)
    def _():
        own_rows.wait()
        xg[PTOK:ROWS, 0:CH] = jnp.concatenate(
            [steps_ref[j].astype(jnp.float32) for j in range(STEPS)], axis=0).astype(jnp.bfloat16)

        for m in (5, 3, 7, 1, 4, 2, 6):
            first_direct(m).start()

        @pl.loop(1, NB)
        def _(b):
            first_copy(b).start()

    lens = [lens_ref[grp, d] for d in range(DOCS)]
    starts = [jnp.int32(0)]
    for d in range(DOCS):
        starts.append(starts[-1] + lens[d])

    def pick(values, index):
        out = jnp.full(index.shape, values[-1], jnp.int32)
        for d in range(DOCS - 1):
            out = jnp.where(index == d, values[d], out)
        return out

    def segment_and_place(row):
        of_prompt = sum((row >= starts[d]).astype(jnp.int32) for d in range(1, DOCS))
        of_step = (row - PTOK) & (DOCS - 1)
        step = (row - PTOK) >> 2
        segment = jnp.where(row < PTOK, of_prompt, of_step)
        place = jnp.where(row < PTOK, row - pick(starts[:DOCS], of_prompt), pick(lens, of_step) + step)
        return jnp.where(row < ROWS, segment, -1), place

    seg_q, place_q = segment_and_place(lax.broadcasted_iota(jnp.int32, (ROWS, HD), 0))
    lane = lax.broadcasted_iota(jnp.int32, (ROWS, HD), 1)
    half = (lane & (HD // 2 - 1)).astype(jnp.float32)
    angle = place_q.astype(jnp.float32) * jnp.exp(half * (-2.0 / HD * math.log(THETA)))
    cosb[...] = jnp.cos(angle)
    sine = jnp.sin(angle)
    sinb[...] = jnp.where(lane < HD // 2, -sine, sine)
    for part in range(KEYS // HD):
        seg_k, place_k = segment_and_place(lax.broadcasted_iota(jnp.int32, (ROWS, HD), 1) + part * HD)
        bias[:, part * HD : (part + 1) * HD] = jnp.where((seg_q == seg_k) & (place_k <= place_q), 0.0, -1e30)
    row = lax.broadcasted_iota(jnp.int32, (N_GRP * STEPS * CAP, STEPS * DOCS), 0)
    col = lax.broadcasted_iota(jnp.int32, (N_GRP * STEPS * CAP, STEPS * DOCS), 1)
    dests = [dest_ref[grp, d] for d in range(DOCS)]
    ranks = [
        sum([(dests[e] == dests[d]).astype(jnp.int32) for e in range(d)], jnp.int32(0)) for d in range(DOCS)
    ]
    doc = col & (DOCS - 1)
    chosen = (
        (pick(dests, doc) == (row >> 3)) & (pick(ranks, doc) == (row & 1)) & ((col >> 2) == ((row >> 1) & 3))
    )
    choice[...] = jnp.where(chosen, 1.0, 0.0).astype(jnp.bfloat16)
    kb[...] = jnp.zeros_like(kb)
    vb[:, 0:HD] = jnp.zeros((KEYS, HD), jnp.bfloat16)
    vb[:, HD:] = jnp.ones((KEYS, HD), jnp.bfloat16)
    for m in range(N_TP):
        for copy in weight_copies(m):
            copy.wait()

    def project_in(b):
        def pass_on():
            @pl.when(b < NB - ahead)
            def _():
                forward(b + ahead)

        total, squared = None, None
        for m in range(N_TP):
            if m == PASS_ON_AT:
                pass_on()
            if m > 1 and m % 2 == 0:
                waiter(xg.at[block(b), slot(m, 2)], rs_send, ag_recv.at[b, m // 2 - 1]).wait_recv()
            values = xg[block(b), m * CH : (m + 1) * CH].astype(jnp.float32)
            squares = values * values
            piece = sum(squares[:, i * HD : (i + 1) * HD] for i in range(CH // HD))
            scaled = (values * gain_ref[:, m * CH : (m + 1) * CH]).astype(jnp.bfloat16)
            product = jnp.dot(scaled, w[m * CH : (m + 1) * CH, :], preferred_element_type=jnp.float32)
            total = product if total is None else total + product
            squared = piece if squared is None else squared + piece
        return total * lax.rsqrt(jnp.sum(squared, axis=-1, keepdims=True) * (1.0 / D) + EPS)

    def attend(b, projected):
        cosine, sine = cosb[block(b)], sinb[block(b)]

        def rotated(values):
            return (values * cosine + pltpu.roll(values, HD // 2, 1) * sine).astype(jnp.bfloat16)

        heads = [rotated(projected[:, h * HD : (h + 1) * HD]) for h in range(HQ + 1)]
        kb[block(b)] = heads[HQ]
        vb[block(b), 0:HD] = projected[:, (HQ + 1) * HD :].astype(jnp.bfloat16)
        queries = jnp.concatenate(heads[:HQ], axis=0)
        scores = lax.dot_general(
            queries, kb[...], (((1,), (1,)), ((), ())), preferred_element_type=jnp.float32)
        scores = scores * (1.0 / math.sqrt(HD)) + jnp.concatenate([bias[block(b)]] * HQ, axis=0)
        raised = jnp.exp(scores - jnp.max(scores, axis=-1, keepdims=True)).astype(jnp.bfloat16)
        mixed = jnp.dot(raised, vb[...], preferred_element_type=jnp.float32)
        mixed = (mixed[:, 0:HD] / mixed[:, HD:]).astype(jnp.bfloat16)
        return jnp.concatenate([mixed[h * R : (h + 1) * R] for h in range(HQ)], axis=1)

    def finish(b):
        waiter(rs.at[:, block(b)], rs_send, rs_recv.at[b]).wait_recv()
        total = own[b % 2] + xg[block(b), 0:CH].astype(jnp.float32)
        for m in range(SLOTS):
            total += rs[m, block(b)].astype(jnp.float32)
        xo[block(b)] = total.astype(jnp.bfloat16)

        @pl.when(phase < N_PHASE - 1)
        def _():
            next_copy(b, 1).start()
            next_copy(b, 0).start()

    def project_out(b, heads):
        def product(m):
            return jnp.dot(heads, wo[:, m * CH : (m + 1) * CH], preferred_element_type=jnp.float32)

        ready = product(0)
        for m in range(SLOTS):
            if m == FINISH_AT:
                pl.when(b > 0)(functools.partial(finish, b - 1))
            following = product(m + 1)
            st[m, block(b)] = ready.astype(jnp.bfloat16)
            part_copy(b, m).start()
            ready = following
        own[b % 2] = ready
        if FINISH_AT == SLOTS:
            pl.when(b > 0)(functools.partial(finish, b - 1))

    forward(0)

    @pl.when(phase == 0)
    def _():
        forward(1)

    @pl.loop(0, NB)
    def _(b):

        projected = project_in(b)
        heads = attend(b, projected)

        @pl.when(b == 0)
        def _():
            for m in range(N_TP):
                out_weight_copy(m).wait()

        project_out(b, heads)


    finish(NB - 1)

    picked = jnp.dot(choice[...], xo[PTOK:ROWS], preferred_element_type=jnp.float32)
    for g in range(N_GRP):
        rows = picked[g * STEPS * CAP : (g + 1) * STEPS * CAP]
        dsend[g] = jnp.concatenate([rows[:, : CH // 2], rows[:, CH // 2 :]], axis=0).astype(jnp.bfloat16)

    def decode_copy(k):
        to = (grp + k) % N_GRP
        return pltpu.make_async_remote_copy(
            src_ref=dsend.at[to], dst_ref=drecv.at[grp],
            send_sem=dec_send.at[k], recv_sem=dec_recv.at[k],
            device_id=(phase, to, me), device_id_type=MESH)

    for k in range(1, N_GRP):
        decode_copy(k).start()
    drecv[grp] = dsend[grp]
    pre_out[...] = xo[0:PTOK]

    @pl.when(phase == 0)
    def _():
        waiter(xg.at[:, slot(0)], first_send, rs_recv.at[0]).wait_send()
        waiter(xg.at[block(0), slot(0, 6)], first_send, rs_recv.at[0]).wait_send()
        waiter(xg.at[pl.ds(R, ROWS - R), slot(0, 6)], ag_send, rs_recv.at[0]).wait_send()

    @pl.when(phase < N_PHASE - 1)
    def _():
        waiter(xg.at[:, slot(0, 2)], next_send, rs_recv.at[0]).wait_send()

    @pl.when(phase > 0)
    def _():
        waiter(xg.at[:, slot(0, 6)], ag_send, rs_recv.at[0]).wait_send()

    waiter(st, rs_send, rs_recv.at[0]).wait_send()

    for k in range(1, N_GRP):
        came = (grp + N_GRP - k) % N_GRP
        pltpu.make_async_remote_copy(
            src_ref=dsend.at[came], dst_ref=drecv.at[came],
            send_sem=dec_send.at[k], recv_sem=dec_recv.at[k],
            device_id=(phase, came, me), device_id_type=MESH).wait_recv()
        decode_copy(k).wait_send()
    n = N_GRP * STEPS * CAP
    row = lax.broadcasted_iota(jnp.int32, (n, 2 * n), 0)
    col = lax.broadcasted_iota(jnp.int32, (n, 2 * n), 1)
    wanted = ((row >> 1) & 3) * 16 + (row >> 3) * 2 + (row & 1)
    received = drecv[...].reshape(2 * n, CH // 2)
    for part in range(2):
        order = jnp.where(col == wanted + part * STEPS * CAP, 1.0, 0.0).astype(jnp.bfloat16)
        arranged = jnp.dot(order, received, preferred_element_type=jnp.float32)
        dec_out[:, :, part * (CH // 2) : (part + 1) * (CH // 2)] = arranged.reshape(
            STEPS, N_GRP * CAP, CH // 2).astype(jnp.bfloat16)


def body(
    prompt_embed, prompt_lengths, decode_group, step_embed, norm_gain, w_query, w_key, w_value, w_out,
):
    vmem = pl.BlockSpec(memory_space=pltpu.VMEM)
    hbm = pl.BlockSpec(memory_space=pl.ANY)
    bf16, f32 = jnp.bfloat16, jnp.float32
    dma = pltpu.SemaphoreType.DMA
    prefill, decode = pl.pallas_call(
        kernel,
        name="layers",
        out_shape=(
            jax.ShapeDtypeStruct((PTOK, CH), bf16),
            jax.ShapeDtypeStruct((STEPS, N_GRP * CAP, CH), bf16),
        ),
        in_specs=[hbm] * 9,
        out_specs=(vmem, vmem),
        scratch_shapes=[
            pltpu.SMEM((N_GRP, DOCS), jnp.int32),
            pltpu.SMEM((N_GRP, DOCS), jnp.int32),
            pltpu.VMEM((STEPS, DOCS, CH), bf16),
            pltpu.VMEM((1, D), f32),
            pltpu.VMEM((D, NQKV), bf16),
            pltpu.VMEM((HQ * HD, D), bf16),
            pltpu.VMEM((ROWS, D), bf16),
            pltpu.VMEM((SLOTS, ROWS, CH), bf16),
            pltpu.VMEM((SLOTS, ROWS, CH), bf16),
            pltpu.VMEM((ROWS, CH), bf16),
            pltpu.VMEM((2, R, CH), f32),
            pltpu.VMEM((N_GRP * STEPS * CAP, STEPS * DOCS), bf16),
            pltpu.VMEM((KEYS, HD), bf16),
            pltpu.VMEM((KEYS, 2 * HD), bf16),
            pltpu.VMEM((ROWS, HD), f32),
            pltpu.VMEM((ROWS, HD), f32),
            pltpu.VMEM((ROWS, KEYS), f32),
            pltpu.VMEM((N_GRP, 2 * STEPS * CAP, CH // 2), bf16),
            pltpu.VMEM((N_GRP, 2 * STEPS * CAP, CH // 2), bf16),
            dma((4,)),
            dma((5, N_TP)),
            dma(()),
            dma(()),
            dma((NB, 2)),
            dma(()),
            dma((NB, len(NEIGHBOURS))),
            dma(()),
            dma((NB,)),
            dma((N_GRP,)),
            dma((N_GRP,)),
        ],
        compiler_params=pltpu.CompilerParams(
            collective_id=0, has_side_effects=True, vmem_limit_bytes=60 << 20),
    )(
        prompt_lengths,
        decode_group.reshape(N_GRP, DOCS),
        prompt_embed,
        step_embed,
        norm_gain,
        w_query[0],
        w_key[0],
        w_value[0],
        w_out[0],
    )
    return prefill[None], decode[None]


def solution(mesh):
    return jax.shard_map(
        body,
        mesh=mesh,
        in_specs=(
            P("grp", "tp"),
            P(),
            P(),
            P(None, "grp", "tp"),
            P("phase", None),
            P("phase", None, "tp"),
            P("phase", None, "tp"),
            P("phase", None, "tp"),
            P("phase", "tp", None),
        ),
        out_specs=(P("phase", "grp", "tp"), P("phase", None, "grp", "tp")),
        check_vma=False,
    )
```

time: 191 us -> 133 us (0.70)
  Pallas kernels: 181 us -> 129 us
  local copies, waits for them, and re-layouts: 8.35 us -> 3.14 us
    pallas_call x1, Pallas kernels: 181 us -> 129 us  [body(): pl.pallas_call(kernel, name='layers', out_shape=(jax.ShapeDtypeStruct((PT...]
    unnamed x14 -> x2, local copies, waits for them, and re-layouts: 7.58 us -> 3.14 us
where the time goes in v2:
time: 133 us
  Pallas kernels  129 us (97%)
  local copies, waits for them, and re-layouts  3.14 us (2%)
    pallas_call x1, Pallas kernels, body(): pl.pallas_call(kernel, name='layers', out_shape=(jax.ShapeDtypeStruct((PT...  129 us
    unnamed x2, local copies, waits for them, and re-layouts  3.14 us

profile of v2, /device:TPU:7, one launch (start us, length us, event | category | flops | bytes accessed | tf_op | source)
XLA Modules:
  0.0 132.8 jit_solution(17061732205091029047)
XLA Ops:
  0.6 129.0 %layers.1 = (bf16[128,1024]{1,0:T(8,128)(2,1)}, bf16[4,8,1024]{2,1,0:T(8,128)(2,1)}) custom-call(s32[4,4]{1,0:T(4,128)} %lens_hbm.1, s32[4,4]{1,0:T(4,128)} %bitcast.13, bf16[128,1024]{1,0:T(8,128)(2,1)} %x_hbm.1, bf16[4,4,1024]{2,1,0:T(4,128)(2,1)} %steps_hbm.1, f32[1,8192]{1,0:T(1,128)} %gain_hbm.1, bf16[8192,512]{1,0:T(8,128)(2,1)} %bitcast.7, ...), custom_call_target="tpu_custom_call" | custom-call | tf_op jit(solution)/shard_map/layers/pallas_call | solution.py:377
  129.6 1.7 %copy.13 = bf16[1,128,1024]{2,1,0:T(8,128)(2,1)} copy(bf16[1,128,1024]{2,1,0:T(8,128)(2,1)} %bitcast.11) | data formatting | bytes 524288
  131.3 1.5 %copy.14 = bf16[1,4,8,1024]{3,2,1,0:T(8,128)(2,1)} copy(bf16[1,4,8,1024]{3,2,1,0:T(8,128)(2,1)} %bitcast.12) | data formatting | bytes 131072

commit v3 on v2

--- a/solution.py
+++ b/solution.py
@@ -29,8 +29,8 @@
 R = 16
 NB = ROWS // R
 SLOTS = N_TP - 1
+SHARE_TO = ((1, 2), (1, 1), (1, 3), (0, 2), (1, 0), (0, 1), (0, 3), (0, 0))
 PASS_ON_AT = 2
-FINISH_AT = 7
 SLOT_FROM = ((0, 0), (1, 2), (0, 1), (1, 3), (0, 3), (1, 1), (1, 0), (0, 2))
 NEIGHBOURS = ((0, 3), (0, 1), (1, 0))
 
@@ -51,7 +51,7 @@
         return ((my_z + row) % 2) * 4 + (my_y + along) % 4
 
     def target(m):
-        return at(1 - m // 4, 7 - m)
+        return at(*SHARE_TO[m])
 
     opposite = at(1, 2)
 
@@ -267,7 +267,7 @@
 
     def finish(b):
         waiter(rs.at[:, block(b)], rs_send, rs_recv.at[b]).wait_recv()
-        total = own[b % 2] + xg[block(b), 0:CH].astype(jnp.float32)
+        total = own[b % 2]
         for m in range(SLOTS):
             total += rs[m, block(b)].astype(jnp.float32)
         xo[block(b)] = total.astype(jnp.bfloat16)
@@ -283,15 +283,11 @@
 
         ready = product(0)
         for m in range(SLOTS):
-            if m == FINISH_AT:
-                pl.when(b > 0)(functools.partial(finish, b - 1))
             following = product(m + 1)
             st[m, block(b)] = ready.astype(jnp.bfloat16)
             part_copy(b, m).start()
             ready = following
-        own[b % 2] = ready
-        if FINISH_AT == SLOTS:
-            pl.when(b > 0)(functools.partial(finish, b - 1))
+        own[b % 2] = ready + xg[block(b), 0:CH].astype(jnp.float32)
 
     forward(0)
 
@@ -311,6 +307,7 @@
                 out_weight_copy(m).wait()
 
         project_out(b, heads)
+        pl.when(b > 0)(functools.partial(finish, b - 1))
 
 
     finish(NB - 1)
@@ -329,6 +326,11 @@
 
     for k in range(1, N_GRP):
         decode_copy(k).start()
+    n = N_GRP * STEPS * CAP
+    row = lax.broadcasted_iota(jnp.int32, (n, 2 * n), 0)
+    col = lax.broadcasted_iota(jnp.int32, (n, 2 * n), 1)
+    wanted = ((row >> 1) & 3) * 16 + (row >> 3) * 2 + (row & 1)
+    orders = [jnp.where(col == wanted + part * STEPS * CAP, 1.0, 0.0).astype(jnp.bfloat16) for part in range(2)]
     drecv[grp] = dsend[grp]
     pre_out[...] = xo[0:PTOK]
 
@@ -355,14 +357,9 @@
             send_sem=dec_send.at[k], recv_sem=dec_recv.at[k],
             device_id=(phase, came, me), device_id_type=MESH).wait_recv()
         decode_copy(k).wait_send()
-    n = N_GRP * STEPS * CAP
-    row = lax.broadcasted_iota(jnp.int32, (n, 2 * n), 0)
-    col = lax.broadcasted_iota(jnp.int32, (n, 2 * n), 1)
-    wanted = ((row >> 1) & 3) * 16 + (row >> 3) * 2 + (row & 1)
     received = drecv[...].reshape(2 * n, CH // 2)
     for part in range(2):
-        order = jnp.where(col == wanted + part * STEPS * CAP, 1.0, 0.0).astype(jnp.bfloat16)
-        arranged = jnp.dot(order, received, preferred_element_type=jnp.float32)
+        arranged = jnp.dot(orders[part], received, preferred_element_type=jnp.float32)
         dec_out[:, :, part * (CH // 2) : (part + 1) * (CH // 2)] = arranged.reshape(
             STEPS, N_GRP * CAP, CH // 2).astype(jnp.bfloat16)
 

time: 133 us -> 132 us (level)
  no operation moved by 1% of the time
where the time goes in v3:
time: 132 us
  Pallas kernels  128 us (97%)
  local copies, waits for them, and re-layouts  3.14 us (2%)
    pallas_call x1, Pallas kernels, body(): pl.pallas_call(kernel, name='layers', out_shape=(jax.ShapeDtypeStruct((PT...  128 us
    unnamed x2, local copies, waits for them, and re-layouts  3.14 us

profile of v3, /device:TPU:7, one launch (start us, length us, event | category | flops | bytes accessed | tf_op | source)
XLA Modules:
  0.0 132.0 jit_solution(12763549661449908390)
XLA Ops:
  0.6 128.2 %layers.1 = (bf16[128,1024]{1,0:T(8,128)(2,1)}, bf16[4,8,1024]{2,1,0:T(8,128)(2,1)}) custom-call(s32[4,4]{1,0:T(4,128)} %lens_hbm.1, s32[4,4]{1,0:T(4,128)} %bitcast.13, bf16[128,1024]{1,0:T(8,128)(2,1)} %x_hbm.1, bf16[4,4,1024]{2,1,0:T(4,128)(2,1)} %steps_hbm.1, f32[1,8192]{1,0:T(1,128)} %gain_hbm.1, bf16[8192,512]{1,0:T(8,128)(2,1)} %bitcast.7, ...), custom_call_target="tpu_custom_call" | custom-call | tf_op jit(solution)/shard_map/layers/pallas_call | solution.py:374
  128.8 1.7 %copy.13 = bf16[1,128,1024]{2,1,0:T(8,128)(2,1)} copy(bf16[1,128,1024]{2,1,0:T(8,128)(2,1)} %bitcast.11) | data formatting | bytes 524288
  130.5 1.5 %copy.14 = bf16[1,4,8,1024]{3,2,1,0:T(8,128)(2,1)} copy(bf16[1,4,8,1024]{3,2,1,0:T(8,128)(2,1)} %bitcast.12) | data formatting | bytes 131072

commit v4 on v3

--- a/solution.py
+++ b/solution.py
@@ -163,17 +163,19 @@
 
     middle = ((phase > 0) & (phase < N_PHASE - 1)).astype(jnp.int32)
     pl.semaphore_wait(barrier, SLOTS + N_GRP - 1 + 2 + 2 * middle)
+    @pl.when(phase == 0)
+    def _():
+        own_rows.wait()
+        for m in (5, 3, 7, 1, 4, 2, 6):
+            first_direct(m).start()
+
     for copy in small:
         copy.wait()
 
     @pl.when(phase == 0)
     def _():
-        own_rows.wait()
         xg[PTOK:ROWS, 0:CH] = jnp.concatenate(
             [steps_ref[j].astype(jnp.float32) for j in range(STEPS)], axis=0).astype(jnp.bfloat16)
-
-        for m in (5, 3, 7, 1, 4, 2, 6):
-            first_direct(m).start()
 
         @pl.loop(1, NB)
         def _(b):

time: 132 us -> 131 us (level)
  no operation moved by 1% of the time
where the time goes in v4:
time: 131 us
  Pallas kernels  127 us (97%)
  local copies, waits for them, and re-layouts  3.14 us (2%)
    pallas_call x1, Pallas kernels, body(): pl.pallas_call(kernel, name='layers', out_shape=(jax.ShapeDtypeStruct((PT...  127 us
    unnamed x2, local copies, waits for them, and re-layouts  3.14 us

profile of v4, /device:TPU:7, one launch (start us, length us, event | category | flops | bytes accessed | tf_op | source)
XLA Modules:
  0.0 131.1 jit_solution(3370036746108574467)
XLA Ops:
  0.6 127.3 %layers.1 = (bf16[128,1024]{1,0:T(8,128)(2,1)}, bf16[4,8,1024]{2,1,0:T(8,128)(2,1)}) custom-call(s32[4,4]{1,0:T(4,128)} %lens_hbm.1, s32[4,4]{1,0:T(4,128)} %bitcast.13, bf16[128,1024]{1,0:T(8,128)(2,1)} %x_hbm.1, bf16[4,4,1024]{2,1,0:T(4,128)(2,1)} %steps_hbm.1, f32[1,8192]{1,0:T(1,128)} %gain_hbm.1, bf16[8192,512]{1,0:T(8,128)(2,1)} %bitcast.7, ...), custom_call_target="tpu_custom_call" | custom-call | tf_op jit(solution)/shard_map/layers/pallas_call | solution.py:376
  127.9 1.7 %copy.13 = bf16[1,128,1024]{2,1,0:T(8,128)(2,1)} copy(bf16[1,128,1024]{2,1,0:T(8,128)(2,1)} %bitcast.11) | data formatting | bytes 524288
  129.6 1.5 %copy.14 = bf16[1,4,8,1024]{3,2,1,0:T(8,128)(2,1)} copy(bf16[1,4,8,1024]{3,2,1,0:T(8,128)(2,1)} %bitcast.12) | data formatting | bytes 131072
